TPU v7x, 32 devices: a whole 2x2x4 slice. The times are simulated.
32 devices in a mesh: seq: 8 (over y, x, core), head: 4 (over z).
Axes of the slice: x: 2, y: 2, z: 4, core: 2. Of those that a mesh axis runs over, the one named last changes fastest.
Arguments:
- hidden: bfloat16 [12288, 4096], P('seq', 'head'), may hold values from -6 to 6
- norm_gain: float32 [4096], replicated, may hold values from 0.1 to 1.9
- w_query: bfloat16 [4096, 4096], P(None, 'head'), may hold values from -0.09375 to 0.09375
- w_out: bfloat16 [4096, 4096], P('head'), may hold values from -0.5 to 0.5
- keys: bfloat16 [12288, 1024], P('seq', 'head'), may hold values from -240 to 240
- values: bfloat16 [12288, 1024], P('seq', 'head'), may hold values from -6 to 6
- cand_count: int32 [8], P('seq'), may hold values from 1 to 384, 768 in all
- cand_pos: int32 [3072], P('seq'), may hold values from 0 to 1535, as said below
Outputs:
- slot_update: bfloat16 [3072, 4096], P('seq', 'head')
Inputs may be any that keep to these rules, and one draw needn't show every extreme that they name: `cand_pos`: each shard's 384 slots hold distinct positions within that shard; its first cand_count slots are the used ones. `cand_count`: the counts sum to 768.
All inputs are finite; a program needn't handle non-finite values. No bound on the sum of `cand_count` on one device may be relied on, other than what follows from the above.
Results may differ from a plain program's by a relative error of at most 0.019.
The roundings to bfloat16 on the way count: a program that leaves them out, or rounds other values in their place, can miss the bound.
Values may be sent and summed in bfloat16 or wider, within the bound.
A program may use at most 128 MiB of HBM per device.

v0:
```python
import math

import jax
import jax.numpy as jnp
from jax import lax
from jax.sharding import PartitionSpec as P

HEAD_SIZE = 128
M_DEV = 96


EPS = 1e-05
ROPE_BASE = 500000.0
NEG_FLOOR = -1e30


def carried_in(value, axis, join, neutral):
    count, mine = (lax.axis_size(axis), lax.axis_index(axis))
    pieces = lax.all_gather(value, axis)
    so_far = jnp.full_like(value, 0) + jnp.asarray(neutral, value.dtype)

    def turn(position, so_far):
        longer = join(so_far, pieces[position])
        return jnp.where(position < mine, longer, so_far)

    return lax.fori_loop(0, count - 1, turn, so_far)


def add_ints(earlier, later):
    return earlier + later


def rotate(query_rows, positions, head_dim):
    half_dim = head_dim // 2
    inverse_freq = jnp.exp(
        -math.log(ROPE_BASE) * 2.0 * jnp.arange(half_dim, dtype=jnp.float32) / head_dim
    )
    angles = positions.astype(jnp.float32)[:, None] * inverse_freq[None, :]
    cosine = jnp.cos(angles)[:, None, :]
    sine_part = jnp.sin(angles)[:, None, :]
    first_half = query_rows[..., :half_dim]
    second_half = query_rows[..., half_dim:]
    return jnp.concatenate(
        [
            first_half * cosine - second_half * sine_part,
            second_half * cosine + first_half * sine_part,
        ],
        axis=-1,
    )


def body(hidden, norm_gain, w_query, w_out, keys, values, cand_count, cand_pos):
    shards = lax.axis_size("seq")
    seq_dev, width_dev = hidden.shape
    slot_count = cand_pos.shape[0]
    bucket = slot_count // shards
    head_dim = HEAD_SIZE
    kv_local = keys.shape[1] // head_dim
    q_local = w_query.shape[1] // head_dim
    repeat = q_local // kv_local
    seq_index = lax.axis_index("seq")
    live_count = cand_count[0]
    offset = carried_in(cand_count, "seq", add_ints, jnp.zeros((1,), jnp.int32))[0]
    owner_ids = jnp.arange(shards, dtype=jnp.int32)[:, None]
    depth_ids = jnp.arange(bucket, dtype=jnp.int32)[None, :]
    slot_ids = depth_ids * shards + (owner_ids - offset) % shards
    is_live = slot_ids < live_count
    local_slots = cand_pos[slot_ids]
    send_rows = jnp.where(is_live[..., None], hidden[local_slots], jnp.zeros((), hidden.dtype))
    send_ids = jnp.where(is_live, offset + slot_ids, -1)
    send_pos = jnp.where(is_live, seq_index * seq_dev + local_slots, -1)
    got_rows, got_ids, got_pos = (
        lax.all_to_all(send_rows, "seq", split_axis=0, concat_axis=0, tiled=True),
        lax.all_to_all(send_ids, "seq", split_axis=0, concat_axis=0, tiled=True),
        lax.all_to_all(send_pos, "seq", split_axis=0, concat_axis=0, tiled=True),
    )
    flat_ids = got_ids.reshape(-1)
    target = jnp.where(flat_ids >= 0, flat_ids // shards, -1)
    row_range = jnp.arange(M_DEV, dtype=jnp.int32)
    placing = target[None, :] == row_range[:, None]
    local_rows = jnp.dot(
        placing.astype(jnp.bfloat16),
        got_rows.reshape(-1, width_dev),
        preferred_element_type=jnp.float32,
    ).astype(jnp.bfloat16)
    local_pos = jnp.sum(jnp.where(placing, got_pos.reshape(-1)[None, :], 0), axis=1).astype(
        jnp.int32
    )
    features_full = lax.all_gather(local_rows, "head", axis=1, tiled=True)
    widened = features_full.astype(jnp.float32)
    inv_rms = lax.rsqrt(jnp.mean(widened * widened, axis=1, keepdims=True) + EPS)
    normed = (widened * inv_rms * norm_gain).astype(jnp.bfloat16)
    query_rows = jnp.dot(normed, w_query, preferred_element_type=jnp.float32).reshape(
        M_DEV, q_local, head_dim
    )
    query_rows = (rotate(query_rows, local_pos, head_dim) * (1.0 / math.sqrt(head_dim))).astype(
        jnp.bfloat16
    )
    grouped_heads = query_rows.reshape(M_DEV, kv_local, repeat, head_dim)
    last_pos = jnp.max(local_pos)
    initial = (
        jnp.full((M_DEV, kv_local, repeat), NEG_FLOOR, jnp.float32),
        jnp.zeros((M_DEV, kv_local, repeat), jnp.float32),
        jnp.zeros((M_DEV, kv_local, repeat, head_dim), jnp.float32),
    )
    key_view = keys.reshape(seq_dev, kv_local, head_dim)
    value_view = values.reshape(seq_dev, kv_local, head_dim)
    key_piece = lax.all_gather(key_view, "seq", axis=0, tiled=True)
    value_piece = lax.all_gather(value_view, "seq", axis=0, tiled=True)
    piece_rows = key_piece.shape[0]
    block_len = math.gcd(piece_rows, 512)
    key_blocks = key_piece.reshape(piece_rows // block_len, block_len, kv_local, head_dim)
    value_blocks = value_piece.reshape(piece_rows // block_len, block_len, kv_local, head_dim)
    block_starts = block_len * jnp.arange(piece_rows // block_len, dtype=jnp.int32)

    def fold_step(running, block_item):
        key_block, value_block, block_first = block_item

        def compute(_):
            peak_run, denominator, numerator = running
            scores = jnp.einsum(
                "mgrd,ngd->mgrn", grouped_heads, key_block, preferred_element_type=jnp.float32
            )
            key_pos = block_first + jnp.arange(block_len, dtype=jnp.int32)
            visible = key_pos[None, None, None, :] <= local_pos[:, None, None, None]
            scores = jnp.where(visible, scores, -jnp.inf)
            peak_new = jnp.maximum(peak_run, jnp.max(scores, axis=3))
            factor = jnp.exp(peak_run - peak_new)
            weight = jnp.exp(scores - peak_new[..., None])
            denominator = denominator * factor + jnp.sum(weight, axis=3)
            numerator = numerator * factor[..., None] + jnp.einsum(
                "mgrn,ngd->mgrd",
                weight.astype(jnp.bfloat16),
                value_block,
                preferred_element_type=jnp.float32,
            )
            return (peak_new, denominator, numerator)

        def skipped(_):
            return running

        return (lax.cond(block_first > last_pos, skipped, compute, None), None)

    result_state, _ = lax.scan(fold_step, initial, (key_blocks, value_blocks, block_starts))
    peak_run, denominator, numerator = result_state
    mixed_heads = (
        (numerator / denominator[..., None]).reshape(M_DEV, q_local * head_dim).astype(jnp.bfloat16)
    )
    partial_out = jnp.dot(mixed_heads, w_out, preferred_element_type=jnp.float32)
    update = lax.psum_scatter(
        partial_out.astype(jnp.bfloat16), "head", scatter_dimension=1, tiled=True
    )
    placing_back = target[:, None] == row_range[None, :]
    send_back = jnp.dot(
        placing_back.astype(jnp.bfloat16), update, preferred_element_type=jnp.float32
    ).astype(jnp.bfloat16)
    returned = lax.all_to_all(
        send_back.reshape(shards, bucket, width_dev), "seq", split_axis=0, concat_axis=0, tiled=True
    )
    slot_all = jnp.arange(slot_count, dtype=jnp.int32)
    source_index = (offset + slot_all % shards) % shards * bucket + slot_all // shards
    result = returned.reshape(slot_count, width_dev)[source_index]
    return jnp.where((slot_all < live_count)[:, None], result, jnp.zeros((), jnp.bfloat16))


def solution(mesh):
    in_specs = (
        P("seq", "head"),
        P(),
        P(None, "head"),
        P("head", None),
        P("seq", "head"),
        P("seq", "head"),
        P("seq"),
        P("seq"),
    )
    out_specs = P("seq", "head")
    return jax.shard_map(body, mesh=mesh, in_specs=in_specs, out_specs=out_specs, check_vma=False)
```

profile of v0, /device:TPU:0, one launch (start us, length us, event | category | flops | bytes accessed | tf_op | source)
XLA Modules:
  0.0 331.4 jit_solution(9468264075362709119)
XLA Ops:
  13.4 9.5 %all-reduce = s32[8]{0:T(128)S(1)} all-reduce(s32[8]{0:T(128)S(1)} %dynamic-update-slice), channel_id=2, replica_groups=mesh['seq'=8,'head'=4] {'seq'}, use_global_device_ids=true, to_apply=%add | all-reduce | flops 8 | bytes 64
  22.9 8.7 %while.27 = (s32[]{:T(128)}, s32[1]{0:T(128)}, s32[]{:T(128)}, s32[8,1]{0,1:T(1,128)S(1)}, s32[]{:T(128)}) while((s32[]{:T(128)}, s32[1]{0:T(128)}, s32[]{:T(128)}, s32[8,1]{0,1:T(1,128)S(1)}, s32[]{:T(128)}) %tuple.80), condition=%wide.region_1.2_spmd, body=%wide.region_0.1_spmd.sunk | while | flops 5 | bytes 107 | solution.py:26
  58.0 10.7 %all-to-all-done.2 = bf16[8,48,1024]{2,1,0:T(8,128)(2,1)S(1)} async-done(((bf16[8,48,1024]{2,1,0:T(8,128)(2,1)}), bf16[8,48,1024]{2,1,0:T(8,128)(2,1)S(1)}, u32[]{:S(2)}, u32[]{:S(2)}) %all-to-all-start.2) | async-done | bytes 786464 | tf_op jit(solution)/shard_map/all_to_all | solution.py:73
  69.0 17.9 %all_gather.18 = bf16[96,4096]{1,0:T(8,128)(2,1)S(1)} all-gather(bf16[96,1024]{1,0:T(8,128)(2,1)S(1)} %convolution_convert_fusion.2), channel_id=1, replica_groups=mesh['seq'=8,'head'=4] {'head'}, dimensions={1}, use_global_device_ids=true | all-gather | bytes 983040 | tf_op jit(solution)/shard_map/all_gather | solution.py:89
  87.1 4.9 %convolution_bitcast_fusion.1 = f32[12,8,8,128]{3,1,2,0:T(8,128)S(1)} fusion(bf16[4096,1024]{1,0:T(8,128)(2,1)} %param.16, bf16[96,4096]{1,0:T(8,128)(2,1)S(1)} %all_gather.18, f32[4096]{0:T(1024)S(1)} %copy-done.3, f32[96]{0:T(128)S(1)} %add_rsqrt_fusion), kind=kOutput, calls=%fused_computation.28 | convolution fusion | flops 806879232 | bytes 9585024 | tf_op jit(solution)/shard_map/dot_general | solution.py:93
  92.8 8.6 %copy.26 = bf16[12288,2,128]{2,0,1:T(8,128)(2,1)} copy(bf16[12288,2,128]{0,2,1:T(8,128)(2,1)} %all-gather.4.cloned.1.call-done) | data formatting | bytes 12582912 | tf_op jit(solution)/shard_map/all_gather | solution.py:108
  101.4 6.2 %copy.31 = bf16[24,512,2,128]{3,1,2,0:T(8,128)(2,1)} copy(bf16[24,512,2,128]{3,1,0,2:T(8,128)(2,1)} %bitcast.65) | data formatting | bytes 12582912 | tf_op jit(solution)/shard_map/while | solution.py:144
  107.6 8.6 %copy.30 = bf16[12288,2,128]{2,0,1:T(8,128)(2,1)} copy(bf16[12288,2,128]{0,2,1:T(8,128)(2,1)} %all-gather.6.cloned.1.call-done) | data formatting | bytes 12582912 | tf_op jit(solution)/shard_map/all_gather | solution.py:109
  116.2 6.1 %copy.32 = bf16[24,512,2,128]{3,1,2,0:T(8,128)(2,1)} copy(bf16[24,512,2,128]{3,1,0,2:T(8,128)(2,1)} %bitcast.66) | data formatting | bytes 12582912 | tf_op jit(solution)/shard_map/while | solution.py:144
  122.4 147.3 %while.28 = (s32[]{:T(128)}, f32[96,2,4]{0,2,1:T(4,128)S(1)}, f32[96,2,4]{0,2,1:T(4,128)S(1)}, f32[96,2,4,128]{3,0,2,1:T(8,128)S(1)}, s32[24]{0:T(128)S(1)}, /*i...) while((s32[]{:T(128)}, f32[96,2,4]{0,2,1:T(4,128)S(1)}, ...), condition=%wide.region_10.11_spmd, body=%wide.region_5.10_spmd.sunk | while | flops 203933696 | bytes 6379139 | solution.py:144
  124.3 4.2 %conditional.2 = (f32[96,2,4]{0,2,1:T(4,128)S(1)}, f32[96,2,4]{0,2,1:T(4,128)S(1)}, f32[96,2,4,128]{3,0,2,1:T(8,128)S(1)}) conditional(s32[]{:T(128)} %convert_element_type.71, (s32[]{:T(128)}, s32[96]{0:T(128)S(1)}, bf16[24,512,2,128]{3,1,2,0:T(8,128)(2,1)}, s32[]{:T(128)}, bf16[96,2,4,128]{3,0,2,1:T(8,128)(2,1)S(1)}, ...), branch_computations={%region_6.8_spmd, %region_9.9_spmd} | conditional | flops 203933696 | bytes 6372764 | solution.py:142
  130.4 4.2 %conditional.2 = (f32[96,2,4]{0,2,1:T(4,128)S(1)}, f32[96,2,4]{0,2,1:T(4,128)S(1)}, f32[96,2,4,128]{3,0,2,1:T(8,128)S(1)}) conditional(s32[]{:T(128)} %convert_element_type.71, (s32[]{:T(128)}, s32[96]{0:T(128)S(1)}, bf16[24,512,2,128]{3,1,2,0:T(8,128)(2,1)}, s32[]{:T(128)}, bf16[96,2,4,128]{3,0,2,1:T(8,128)(2,1)S(1)}, ...), branch_computations={%region_6.8_spmd, %region_9.9_spmd} | conditional | flops 203933696 | bytes 6372764 | solution.py:142
  148.8 4.2 %conditional.2 = (f32[96,2,4]{0,2,1:T(4,128)S(1)}, f32[96,2,4]{0,2,1:T(4,128)S(1)}, f32[96,2,4,128]{3,0,2,1:T(8,128)S(1)}) conditional(s32[]{:T(128)} %convert_element_type.71, (s32[]{:T(128)}, s32[96]{0:T(128)S(1)}, bf16[24,512,2,128]{3,1,2,0:T(8,128)(2,1)}, s32[]{:T(128)}, bf16[96,2,4,128]{3,0,2,1:T(8,128)(2,1)S(1)}, ...), branch_computations={%region_6.8_spmd, %region_9.9_spmd} | conditional | flops 203933696 | bytes 6372764 | solution.py:142
  167.3 4.2 %conditional.2 = (f32[96,2,4]{0,2,1:T(4,128)S(1)}, f32[96,2,4]{0,2,1:T(4,128)S(1)}, f32[96,2,4,128]{3,0,2,1:T(8,128)S(1)}) conditional(s32[]{:T(128)} %convert_element_type.71, (s32[]{:T(128)}, s32[96]{0:T(128)S(1)}, bf16[24,512,2,128]{3,1,2,0:T(8,128)(2,1)}, s32[]{:T(128)}, bf16[96,2,4,128]{3,0,2,1:T(8,128)(2,1)S(1)}, ...), branch_computations={%region_6.8_spmd, %region_9.9_spmd} | conditional | flops 203933696 | bytes 6372764 | solution.py:142
  179.5 4.2 %conditional.2 = (f32[96,2,4]{0,2,1:T(4,128)S(1)}, f32[96,2,4]{0,2,1:T(4,128)S(1)}, f32[96,2,4,128]{3,0,2,1:T(8,128)S(1)}) conditional(s32[]{:T(128)} %convert_element_type.71, (s32[]{:T(128)}, s32[96]{0:T(128)S(1)}, bf16[24,512,2,128]{3,1,2,0:T(8,128)(2,1)}, s32[]{:T(128)}, bf16[96,2,4,128]{3,0,2,1:T(8,128)(2,1)S(1)}, ...), branch_computations={%region_6.8_spmd, %region_9.9_spmd} | conditional | flops 203933696 | bytes 6372764 | solution.py:142
  198.0 4.2 %conditional.2 = (f32[96,2,4]{0,2,1:T(4,128)S(1)}, f32[96,2,4]{0,2,1:T(4,128)S(1)}, f32[96,2,4,128]{3,0,2,1:T(8,128)S(1)}) conditional(s32[]{:T(128)} %convert_element_type.71, (s32[]{:T(128)}, s32[96]{0:T(128)S(1)}, bf16[24,512,2,128]{3,1,2,0:T(8,128)(2,1)}, s32[]{:T(128)}, bf16[96,2,4,128]{3,0,2,1:T(8,128)(2,1)S(1)}, ...), branch_computations={%region_6.8_spmd, %region_9.9_spmd} | conditional | flops 203933696 | bytes 6372764 | solution.py:142
  216.4 4.2 %conditional.2 = (f32[96,2,4]{0,2,1:T(4,128)S(1)}, f32[96,2,4]{0,2,1:T(4,128)S(1)}, f32[96,2,4,128]{3,0,2,1:T(8,128)S(1)}) conditional(s32[]{:T(128)} %convert_element_type.71, (s32[]{:T(128)}, s32[96]{0:T(128)S(1)}, bf16[24,512,2,128]{3,1,2,0:T(8,128)(2,1)}, s32[]{:T(128)}, bf16[96,2,4,128]{3,0,2,1:T(8,128)(2,1)S(1)}, ...), branch_computations={%region_6.8_spmd, %region_9.9_spmd} | conditional | flops 203933696 | bytes 6372764 | solution.py:142
  228.7 4.2 %conditional.2 = (f32[96,2,4]{0,2,1:T(4,128)S(1)}, f32[96,2,4]{0,2,1:T(4,128)S(1)}, f32[96,2,4,128]{3,0,2,1:T(8,128)S(1)}) conditional(s32[]{:T(128)} %convert_element_type.71, (s32[]{:T(128)}, s32[96]{0:T(128)S(1)}, bf16[24,512,2,128]{3,1,2,0:T(8,128)(2,1)}, s32[]{:T(128)}, bf16[96,2,4,128]{3,0,2,1:T(8,128)(2,1)S(1)}, ...), branch_computations={%region_6.8_spmd, %region_9.9_spmd} | conditional | flops 203933696 | bytes 6372764 | solution.py:142
  247.1 4.2 %conditional.2 = (f32[96,2,4]{0,2,1:T(4,128)S(1)}, f32[96,2,4]{0,2,1:T(4,128)S(1)}, f32[96,2,4,128]{3,0,2,1:T(8,128)S(1)}) conditional(s32[]{:T(128)} %convert_element_type.71, (s32[]{:T(128)}, s32[96]{0:T(128)S(1)}, bf16[24,512,2,128]{3,1,2,0:T(8,128)(2,1)}, s32[]{:T(128)}, bf16[96,2,4,128]{3,0,2,1:T(8,128)(2,1)S(1)}, ...), branch_computations={%region_6.8_spmd, %region_9.9_spmd} | conditional | flops 203933696 | bytes 6372764 | solution.py:142
  265.5 4.2 %conditional.2 = (f32[96,2,4]{0,2,1:T(4,128)S(1)}, f32[96,2,4]{0,2,1:T(4,128)S(1)}, f32[96,2,4,128]{3,0,2,1:T(8,128)S(1)}) conditional(s32[]{:T(128)} %convert_element_type.71, (s32[]{:T(128)}, s32[96]{0:T(128)S(1)}, bf16[24,512,2,128]{3,1,2,0:T(8,128)(2,1)}, s32[]{:T(128)}, bf16[96,2,4,128]{3,0,2,1:T(8,128)(2,1)S(1)}, ...), branch_computations={%region_6.8_spmd, %region_9.9_spmd} | conditional | flops 203933696 | bytes 6372764 | solution.py:142
  270.2 5.7 %convolution_convert_fusion = bf16[96,4096]{1,0:T(8,128)(2,1)} fusion(bf16[96,1024]{1,0:T(8,128)(2,1)S(1)} %convert_element_type.48, bf16[1024,4096]{1,0:T(8,128)(2,1)} %param.17), kind=kOutput, calls=%fused_computation.21 | convolution fusion | flops 805699584 | bytes 9371648 | tf_op jit(solution)/shard_map/dot_general | solution.py:149
  275.9 23.0 %reduce-scatter.2.cloned.1.call-done = bf16[96,1024]{1,0:T(8,128)(2,1)} async-done(((bf16[96,4096]{1,0:T(8,128)(2,1)}), bf16[96,1024]{1,0:T(8,128)(2,1)}) %reduce-scatter.2.cloned.1.call-update) | async-done | bytes 196624 | tf_op jit(solution)/shard_map/reduce_scatter | solution.py:150
  305.4 12.6 %all-to-all-done.3 = bf16[8,48,1024]{2,1,0:T(8,128)(2,1)} async-done(((bf16[8,48,1024]{2,1,0:T(8,128)(2,1)}), bf16[8,48,1024]{2,1,0:T(8,128)(2,1)}, u32[]{:S(2)}, u32[]{:S(2)}) %all-to-all-start.3) | async-done | bytes 786464 | tf_op jit(solution)/shard_map/all_to_all | solution.py:157
  318.0 4.8 %gather_fusion.2 = bf16[384,1024]{1,0:T(8,128)(2,1)} fusion(bf16[384,1024]{1,0:T(8,128)(2,1)} %bitcast.24, s32[1024]{0:T(1024)S(1)} %pad_clamp_fusion), kind=kCustom, calls=%fused_computation.2 | custom fusion | bytes 1574400 | tf_op jit(solution)/shard_map/gather | solution.py:162
  (312 shorter events, 221.5 us)
Async XLA Ops:
  6.5 32.3 %copy-start = (bf16[1536,1024]{1,0:T(8,128)(2,1)S(1)}, bf16[1536,1024]{1,0:T(8,128)(2,1)}, u32[]{:S(2)}) copy-start(bf16[1536,1024]{1,0:T(8,128)(2,1)} %param.14) | copy-start | bytes 9437188
  6.5 86.2 %all-gather.4.cloned.1.call-start = ((), (), s32[]{:S(2)}) async-start(), calls=%async_computation.5 | async-start | bytes 7077888 | tf_op jit(solution)/shard_map/all_gather | solution.py:108
  9.0 3.1 copy-start.4
  9.0 22.8 %copy-start.2 = (s32[384]{0:T(512)S(1)}, s32[384]{0:T(512)}, u32[]{:S(2)}) copy-start(s32[384]{0:T(512)} %param.21) | copy-start | bytes 4612
  9.0 98.6 %all-gather.6.cloned.1.call-start = ((), (), s32[]{:S(2)}) async-start(), calls=%async_computation.6 | async-start | bytes 7077888 | tf_op jit(solution)/shard_map/all_gather | solution.py:109
  35.4 8.4 %all-to-all-start = ((s32[8,1,48]{2,1,0:T(1,128)}), s32[8,1,48]{2,1,0:T(1,128)S(1)}, u32[]{:S(2)}, u32[]{:S(2)}) async-start(s32[8,1,48]{2,1,0:T(1,128)} %get-tuple-element.289), calls=%async_computation | async-start | bytes 8192 | tf_op jit(solution)/shard_map/all_to_all | solution.py:74
  43.8 8.8 %all-to-all-start.1 = ((s32[8,1,48]{2,1,0:T(1,128)}), s32[8,1,48]{2,1,0:T(1,128)S(1)}, u32[]{:S(2)}, u32[]{:S(2)}) async-start(s32[8,1,48]{2,1,0:T(1,128)} %get-tuple-element.290), calls=%async_computation.1 | async-start | bytes 8192 | tf_op jit(solution)/shard_map/all_to_all | solution.py:75
  52.6 16.1 %all-to-all-start.2 = ((bf16[8,48,1024]{2,1,0:T(8,128)(2,1)}), bf16[8,48,1024]{2,1,0:T(8,128)(2,1)S(1)}, u32[]{:S(2)}, u32[]{:S(2)}) async-start(bf16[8,48,1024]{2,1,0:T(8,128)(2,1)} %broadcast_select_fusion.1), calls=%async_computation.2 | async-start | bytes 1572864 | tf_op jit(solution)/shard_map/all_to_all | solution.py:73
  56.2 31.0 %copy-start.3 = (f32[4096]{0:T(1024)S(1)}, f32[4096]{0:T(1024)}, u32[]{:S(2)}) copy-start(f32[4096]{0:T(1024)} %param.15) | copy-start | bytes 49156
  56.2 242.8 %reduce-scatter.2.cloned.1.call-start = ((), (), s32[]{:S(2)}) async-start(), calls=%async_computation.7 | async-start | bytes 983040 | tf_op jit(solution)/shard_map/reduce_scatter | solution.py:150
  301.2 16.8 %all-to-all-start.3 = ((bf16[8,48,1024]{2,1,0:T(8,128)(2,1)}), bf16[8,48,1024]{2,1,0:T(8,128)(2,1)}, u32[]{:S(2)}, u32[]{:S(2)}) async-start(bf16[8,48,1024]{2,1,0:T(8,128)(2,1)} %bitcast.23), calls=%async_computation.4 | async-start | bytes 1572864 | tf_op jit(solution)/shard_map/all_to_all | solution.py:157
  318.0 6.9 %copy-start.1 = (bf16[1536,1024]{1,0:T(8,128)(2,1)S(1)}, bf16[1536,1024]{1,0:T(8,128)(2,1)}, u32[]{:S(2)}) copy-start(bf16[1536,1024]{1,0:T(8,128)(2,1)} %param.14) | copy-start | bytes 9437188
Sparse Core Ops, SparseCore 0:
  9.3 48.4 all-gather.3
  59.6 45.4 all-gather.5
  276.0 22.8 reduce-scatter.1
where the time goes:
time: 334 us; the launch traced here: 331 us
  matrix products  82.2 us (25%)
  local copies, waits for them, and re-layouts  65.8 us (20%)
  waiting for transfers between devices  49.8 us (15%)
  other arithmetic  40.3 us (12%)
  loops' own time  36.8 us (11%)
  blocking collectives  27.4 us (8%)
  starting transfers between devices  15.2 us (5%)
  between operations  14 us (4%)
    dot_general x24, matrix products, compute(): jnp.einsum('mgrn,ngd->mgrd', weight.astype(jnp.bfloat16), value_block, pr...  35.2 us
    dot_general x24, matrix products, compute(): jnp.einsum('mgrd,ngd->mgrn', grouped_heads, key_block, preferred_element_...  33.8 us
    another operation x1, loops' own time, body(): lax.scan(fold_step, initial, (key_blocks, value_blocks, block_starts))  31.2 us
    reduce_scatter x1, waiting for transfers between devices, body(): lax.psum_scatter(partial_out.astype(jnp.bfloat16), 'head', scatter_dimens...  23 us
    all_gather x1, blocking collectives, body(): features_full = lax.all_gather(local_rows, 'head', axis=1, tiled=True)  17.9 us
    add x24, other arithmetic, compute(): key_pos = block_first + jnp.arange(block_len, dtype=jnp.int32)  15.6 us
    dynamic_slice x24, local copies, waits for them, and re-layouts, body(): lax.scan(fold_step, initial, (key_blocks, value_blocks, block_starts))  14.1 us
    reduce_sum x24, other arithmetic, compute(): denominator = denominator * factor + jnp.sum(weight, axis=3)  13.6 us
  transfers between devices with their start and end apart: 7, of which 4 were waited for; matrix products, arithmetic and copies ran while one was open for 12% of the time, Pallas kernels for 0%

commit v1 on v0

v1 whole, which is shorter than its diff:
```python
import functools
import math

import jax
import jax.numpy as jnp
from jax import lax
from jax.experimental import pallas as pl
from jax.experimental.pallas import tpu as pltpu
from jax.sharding import PartitionSpec as P

HEAD_SIZE = 128
M_DEV = 96
LANES = 128
TILE = 256

EPS = 1e-05
ROPE_BASE = 500000.0
NEG_FLOOR = -1e30
MESH = pl.DeviceIdType.MESH
F32 = jnp.float32
BF16 = jnp.bfloat16
I32 = jnp.int32


def iota(shape, dim):
    return lax.broadcasted_iota(I32, shape, dim)


def flip_bits(index, step, count):
    out, bit = 0, 1
    while bit < count:
        out = out + bit * (((index // bit) % 2 + (step // bit) % 2) % 2)
        bit *= 2
    return out


def kernel(
    n, nh, bucket,
    meta_ref, hidden_ref, gain_ref, wq_ref, wo_ref, key_ref, val_ref,
    out_ref,
    hid, wq, wo, kbuf, vbuf, vext,
    meta_all, onehot, send_rows, recv_rows, feats, normed, q_all,
    o_send, ml_send, o_recv, ml_recv, mixed, part_send, part_recv, upd, back_send, back_recv,
    load_sem, meta_s, meta_r, rows_s, rows_r, feat_s, feat_r, q_s, q_r,
    o_s, o_r, ml_s, ml_r, part_s, part_r, back_s, back_r,
):
    seq_dev, width = hid.shape
    slots = meta_ref.shape[1] - LANES
    kv_local = key_ref.shape[1] // HEAD_SIZE
    q_cols = wq.shape[1]
    q_local = q_cols // HEAD_SIZE
    repeat = q_local // kv_local
    shift = int(math.log2(n))
    entries = n * bucket
    me = lax.axis_index("seq")
    hme = lax.axis_index("head")

    def load(i, src, dst):
        return pltpu.make_async_copy(src, dst, load_sem.at[i])

    loads = [
        load(0, hidden_ref, hid), load(1, wq_ref, wq), load(2, key_ref, kbuf),
        load(3, val_ref, vbuf), load(4, wo_ref, wo),
    ]
    for copy in loads:
        copy.start()

    barrier = pltpu.get_barrier_semaphore()
    for step in range(1, n):
        pl.semaphore_signal(
            barrier, inc=1, device_id=(flip_bits(me, step, n), hme), device_id_type=MESH
        )
    for step in range(1, nh):
        pl.semaphore_signal(
            barrier, inc=1, device_id=(me, (hme + step) % nh), device_id_type=MESH
        )
    pl.semaphore_wait(barrier, n - 1 + nh - 1)

    def to_seq(src, dst, send, recv, peer):
        return pltpu.make_async_remote_copy(
            src_ref=src, dst_ref=dst.at[me], send_sem=send.at[peer], recv_sem=recv.at[me],
            device_id=(peer, hme), device_id_type=MESH,
        )

    def from_seq(src, dst, send, recv, peer):
        return pltpu.make_async_remote_copy(
            src_ref=src, dst_ref=dst.at[peer], send_sem=send.at[peer], recv_sem=recv.at[peer],
            device_id=(peer, hme), device_id_type=MESH,
        )

    def to_head(src, dst, send, recv, peer):
        return pltpu.make_async_remote_copy(
            src_ref=src, dst_ref=dst.at[hme], send_sem=send.at[peer], recv_sem=recv.at[hme],
            device_id=(me, peer), device_id_type=MESH,
        )

    def from_head(src, dst, send, recv, peer):
        return pltpu.make_async_remote_copy(
            src_ref=src, dst_ref=dst.at[peer], send_sem=send.at[peer], recv_sem=recv.at[peer],
            device_id=(me, peer), device_id_type=MESH,
        )

    peers = [flip_bits(me, step, n) for step in range(1, n)]
    heads = [(hme + step) % nh for step in range(1, nh)]
    for peer in peers:
        to_seq(meta_ref, meta_all, meta_s, meta_r, peer).start()
    meta_all[me] = meta_ref[...]
    for peer in peers:
        from_seq(meta_ref, meta_all, meta_s, meta_r, peer).wait_recv()

    counts = [meta_all[s, 0:1, slots : slots + 1] for s in range(n)]
    offs, total = [], jnp.zeros((1, 1), I32)
    my_off = jnp.zeros((1, 1), I32)
    my_count = meta_ref[0:1, slots : slots + 1]
    for s in range(n):
        offs.append(total)
        my_off = my_off + counts[s] * jnp.where(me > s, 1, 0)
        total = total + counts[s]

    loads[0].wait()
    my_pos = meta_ref[0:1, 0:slots]
    for d in range(n):
        slot = iota((bucket, slots), 0) * n + ((d - my_off) & (n - 1))
        at = jnp.where(iota((bucket, slots), 1) == slot, my_pos, 0).astype(F32)
        place = jnp.sum(at, axis=1, keepdims=True)
        token = iota((bucket, seq_dev), 1).astype(F32)
        onehot[d * bucket : (d + 1) * bucket, :] = jnp.where(token == place, 1.0, 0.0).astype(BF16)

    def pick(t, _):
        cols = pl.ds(pl.multiple_of(t * TILE, TILE), TILE)
        rows = jnp.dot(onehot[...], hid[:, cols], preferred_element_type=F32)
        send_rows[:, :, cols] = rows.astype(BF16).reshape(n, bucket, TILE)
        return 0

    lax.fori_loop(0, width // TILE, pick, 0)
    for peer in peers:
        to_seq(send_rows.at[peer], recv_rows, rows_s, rows_r, peer).start()
    recv_rows[me] = send_rows[me]

    def bucket_of(s, d):
        first = (d - offs[s]) & (n - 1)
        return (offs[s] + first) >> shift, first

    row_m = iota((M_DEV, entries), 0)
    lane_e = iota((M_DEV, entries), 1)
    placing = jnp.zeros((M_DEV, entries), F32)
    for s in range(n):
        base, first = bucket_of(s, me)
        k = lane_e - s * bucket
        hit = (k >= 0) & (k < bucket) & (row_m == base + k) & (k * n + first < counts[s])
        placing = jnp.where(hit, 1.0, placing)
    placing = placing.astype(BF16)

    def positions(d):
        row = iota((M_DEV, slots), 0) * n + d
        lane = iota((M_DEV, slots), 1)
        found = jnp.zeros((M_DEV, slots), I32)
        for s in range(n):
            hit = (lane + offs[s] == row) & (lane < counts[s])
            found = jnp.where(hit, meta_all[s, 0:1, 0:slots] + s * seq_dev, found)
        return jnp.sum(found.astype(F32), axis=1, keepdims=True)

    lane = iota((M_DEV, LANES), 1)
    half = HEAD_SIZE // 2
    freq = jnp.exp(
        (-math.log(ROPE_BASE) * 2.0 / HEAD_SIZE) * (lane % half).astype(F32)
    )
    angle = positions(me) * freq
    cosine = jnp.cos(angle)
    sine = jnp.where(lane < half, -jnp.sin(angle), jnp.sin(angle))
    loads[3].wait()
    for g in range(kv_local):
        vext[g, :, 0:HEAD_SIZE] = vbuf[:, g * HEAD_SIZE : (g + 1) * HEAD_SIZE]
        vext[g, :, HEAD_SIZE : 2 * HEAD_SIZE] = jnp.ones((seq_dev, HEAD_SIZE), BF16)

    for peer in peers:
        from_seq(send_rows.at[peer], recv_rows, rows_s, rows_r, peer).wait_recv()
    gathered = recv_rows[...].reshape(entries, width)
    feats[hme] = jnp.dot(placing, gathered, preferred_element_type=F32).astype(BF16)

    for peer in heads:
        to_head(feats.at[hme], feats, feat_s, feat_r, peer).start()
    for peer in heads:
        from_head(feats.at[hme], feats, feat_s, feat_r, peer).wait_recv()
    square = jnp.zeros((M_DEV, 1), F32)
    for h in range(nh):
        wide = feats[h].astype(F32)
        square = square + jnp.sum(wide * wide, axis=1, keepdims=True)
    inv_rms = lax.rsqrt(square * (1.0 / (nh * width)) + EPS)
    for h in range(nh):
        gain = gain_ref[0:1, h * width : (h + 1) * width]
        normed[:, h * width : (h + 1) * width] = (
            feats[h].astype(F32) * inv_rms * gain
        ).astype(BF16)

    loads[1].wait()
    scale = 1.0 / math.sqrt(HEAD_SIZE)

    def project(t, _):
        cols = pl.ds(pl.multiple_of(t * TILE, TILE), TILE)
        raw = jnp.dot(normed[...], wq[:, cols], preferred_element_type=F32)
        turned = []
        for i in range(TILE // HEAD_SIZE):
            one = raw[:, i * HEAD_SIZE : (i + 1) * HEAD_SIZE]
            turned.append((one * cosine + pltpu.roll(one, half, 1) * sine) * scale)
        q_all[me, :, cols] = jnp.concatenate(turned, axis=1).astype(BF16)
        return 0

    lax.fori_loop(0, q_cols // TILE, project, 0)
    for peer in peers:
        to_seq(q_all.at[me], q_all, q_s, q_r, peer).start()
    loads[2].wait()

    token = me * seq_dev + iota((1, seq_dev), 1)
    token = token.astype(F32)

    def attend(step, _):
        d = flip_bits(me, step, n)

        pos = positions(d)

        @pl.when(step > 0)
        def _():
            from_seq(q_all.at[me], q_all, q_s, q_r, d).wait_recv()

        hidden_bias = jnp.concatenate([pos] * repeat, axis=0)
        stats = jnp.zeros((M_DEV, LANES), F32)
        for g in range(kv_local):
            rows = jnp.concatenate(
                [
                    q_all[d, :, (g * repeat + i) * HEAD_SIZE : (g * repeat + i + 1) * HEAD_SIZE]
                    for i in range(repeat)
                ],
                axis=0,
            )
            score = lax.dot_general(
                rows, kbuf[:, g * HEAD_SIZE : (g + 1) * HEAD_SIZE],
                (((1,), (1,)), ((), ())), preferred_element_type=F32,
            )
            score = jnp.where(token <= hidden_bias, score, NEG_FLOOR)
            peak = jnp.max(score, axis=1, keepdims=True)
            weight = jnp.exp(score - peak).astype(BF16)
            both = jnp.dot(weight, vext[g], preferred_element_type=F32)
            for i in range(repeat):
                head = g * repeat + i
                part = slice(i * M_DEV, (i + 1) * M_DEV)
                o_send[d, :, head * HEAD_SIZE : (head + 1) * HEAD_SIZE] = (
                    both[part, 0:HEAD_SIZE].astype(BF16)
                )
                stats = jnp.where(lane == head, peak[part], stats)
                stats = jnp.where(lane == q_local + head, both[part, HEAD_SIZE:], stats)
        ml_send[d] = stats

        @pl.when(step > 0)
        def _():
            to_seq(o_send.at[d], o_recv, o_s, o_r, d).start()
            to_seq(ml_send.at[d], ml_recv, ml_s, ml_r, d).start()

        return 0

    lax.fori_loop(0, n, attend, 0)
    o_recv[me] = o_send[me]
    ml_recv[me] = ml_send[me]
    for peer in peers:
        from_seq(ml_send.at[peer], ml_recv, ml_s, ml_r, peer).wait_recv()
        from_seq(o_send.at[peer], o_recv, o_s, o_r, peer).wait_recv()

    top = ml_recv[0]
    for s in range(1, n):
        top = jnp.maximum(top, ml_recv[s])
    denom = jnp.zeros((M_DEV, LANES), F32)
    for s in range(n):
        aligned = pltpu.roll(ml_recv[s], LANES - q_local, 1)
        denom = denom + jnp.exp(ml_recv[s] - top) * aligned
    factor = [jnp.exp(ml_recv[s] - top) / denom for s in range(n)]
    for head in range(q_local):
        cols = slice(head * HEAD_SIZE, (head + 1) * HEAD_SIZE)
        joined = jnp.zeros((M_DEV, HEAD_SIZE), F32)
        for s in range(n):
            joined = joined + factor[s][:, head : head + 1] * o_recv[s, :, cols].astype(F32)
        mixed[:, cols] = joined.astype(BF16)

    loads[4].wait()
    for peer in heads + [hme]:

        def block(t, _):
            cols = pl.ds(pl.multiple_of(t * TILE, TILE), TILE)
            src = pl.ds(pl.multiple_of(peer * width + t * TILE, TILE), TILE)
            part_send[peer, :, cols] = jnp.dot(
                mixed[...], wo[:, src], preferred_element_type=F32
            ).astype(BF16)
            return 0

        lax.fori_loop(0, width // TILE, block, 0)
        if peer is not hme:
            to_head(part_send.at[peer], part_recv, part_s, part_r, peer).start()
    part_recv[hme] = part_send[hme]
    for peer in heads:
        from_head(part_send.at[peer], part_recv, part_s, part_r, peer).wait_recv()
    update = part_recv[0].astype(F32)
    for h in range(1, nh):
        update = update + part_recv[h].astype(F32)
    upd[0:M_DEV, :] = update.astype(BF16)
    upd[M_DEV:, :] = jnp.zeros((upd.shape[0] - M_DEV, width), BF16)

    for s in range(n):
        base, first = bucket_of(s, me)
        k = iota((bucket, LANES), 0)
        hit = (iota((bucket, LANES), 1) == base + k) & (k * n + first < counts[s])
        onehot[s * bucket : (s + 1) * bucket, 0:LANES] = jnp.where(hit, 1.0, 0.0).astype(BF16)
    back = jnp.dot(onehot[:, 0:LANES], upd[...], preferred_element_type=F32)
    back_send[...] = back.astype(BF16).reshape(n, bucket, width)
    for peer in peers:
        to_seq(back_send.at[peer], back_recv, back_s, back_r, peer).start()
    back_recv[me] = back_send[me]
    slot = iota((slots, entries), 0)
    entry = ((slot + my_off) & (n - 1)) * bucket + (slot >> shift)
    hit = (iota((slots, entries), 1) == entry) & (slot < my_count)
    restoring = jnp.where(hit, 1.0, 0.0).astype(BF16)
    for peer in peers:
        from_seq(back_send.at[peer], back_recv, back_s, back_r, peer).wait_recv()
    out_ref[...] = jnp.dot(
        restoring, back_recv[...].reshape(entries, width), preferred_element_type=F32
    ).astype(BF16)

    for peer in peers:
        to_seq(meta_ref, meta_all, meta_s, meta_r, peer).wait_send()
        to_seq(send_rows.at[peer], recv_rows, rows_s, rows_r, peer).wait_send()
        to_seq(q_all.at[me], q_all, q_s, q_r, peer).wait_send()
        to_seq(o_send.at[peer], o_recv, o_s, o_r, peer).wait_send()
        to_seq(ml_send.at[peer], ml_recv, ml_s, ml_r, peer).wait_send()
        to_seq(back_send.at[peer], back_recv, back_s, back_r, peer).wait_send()
    for peer in heads:
        to_head(feats.at[hme], feats, feat_s, feat_r, peer).wait_send()
        to_head(part_send.at[peer], part_recv, part_s, part_r, peer).wait_send()


def body(hidden, norm_gain, w_query, w_out, keys, values, cand_count, cand_pos):
    n, nh = lax.axis_size("seq"), lax.axis_size("head")
    seq_dev, width = hidden.shape
    slots = cand_pos.shape[0]
    bucket = -(-slots // n)
    bucket = -(-bucket // 16) * 16
    entries = n * bucket
    q_cols = w_query.shape[1]
    kv_local = keys.shape[1] // HEAD_SIZE
    meta = jnp.concatenate([cand_pos, jnp.broadcast_to(cand_count, (LANES,))])
    meta = jnp.broadcast_to(meta[None, :], (8, slots + LANES))
    seq_sem, head_sem = pltpu.SemaphoreType.DMA((n,)), pltpu.SemaphoreType.DMA((nh,))
    vmem, hbm = pl.BlockSpec(memory_space=pltpu.VMEM), pl.BlockSpec(memory_space=pl.ANY)
    return pl.pallas_call(
        functools.partial(kernel, n, nh, bucket),
        out_shape=jax.ShapeDtypeStruct((slots, width), BF16),
        in_specs=[vmem, hbm, vmem, hbm, hbm, hbm, hbm],
        out_specs=vmem,
        scratch_shapes=[
            pltpu.VMEM(hidden.shape, BF16),
            pltpu.VMEM(w_query.shape, BF16),
            pltpu.VMEM(w_out.shape, BF16),
            pltpu.VMEM(keys.shape, BF16),
            pltpu.VMEM(values.shape, BF16),
            pltpu.VMEM((kv_local, seq_dev, 2 * HEAD_SIZE), BF16),
            pltpu.VMEM((n, 8, slots + LANES), I32),
            pltpu.VMEM((entries, seq_dev), BF16),
            pltpu.VMEM((n, bucket, width), BF16),
            pltpu.VMEM((n, bucket, width), BF16),
            pltpu.VMEM((nh, M_DEV, width), BF16),
            pltpu.VMEM((M_DEV, nh * width), BF16),
            pltpu.VMEM((n, M_DEV, q_cols), BF16),
            pltpu.VMEM((n, M_DEV, q_cols), BF16),
            pltpu.VMEM((n, M_DEV, LANES), F32),
            pltpu.VMEM((n, M_DEV, q_cols), BF16),
            pltpu.VMEM((n, M_DEV, LANES), F32),
            pltpu.VMEM((M_DEV, q_cols), BF16),
            pltpu.VMEM((nh, M_DEV, width), BF16),
            pltpu.VMEM((nh, M_DEV, width), BF16),
            pltpu.VMEM((LANES, width), BF16),
            pltpu.VMEM((n, bucket, width), BF16),
            pltpu.VMEM((n, bucket, width), BF16),
            pltpu.SemaphoreType.DMA((5,)),
            seq_sem, seq_sem, seq_sem, seq_sem, head_sem, head_sem, seq_sem, seq_sem,
            seq_sem, seq_sem, seq_sem, seq_sem, head_sem, head_sem, seq_sem, seq_sem,
        ],
        compiler_params=pltpu.CompilerParams(
            collective_id=0, has_side_effects=True, vmem_limit_bytes=60 * 1024 * 1024
        ),
        name="routed_attention",
    )(meta, hidden, norm_gain[None, :], w_query, w_out, keys, values)


def solution(mesh):
    in_specs = (
        P("seq", "head"),
        P(),
        P(None, "head"),
        P("head", None),
        P("seq", "head"),
        P("seq", "head"),
        P("seq"),
        P("seq"),
    )
    out_specs = P("seq", "head")
    return jax.shard_map(body, mesh=mesh, in_specs=in_specs, out_specs=out_specs, check_vma=False)
```

time: 334 us -> 121 us (0.36)
  the two profiles are of different devices: /device:TPU:0 before, /device:TPU:25 now
where the time goes in v1:
time: 121 us; the launch traced here: 120 us
  Pallas kernels  116 us (96%)
  local copies, waits for them, and re-layouts  3.36 us (3%)
    pallas_call x1, Pallas kernels, body(): pl.pallas_call(functools.partial(kernel, n, nh, bucket), out_shape=jax.Sh...  116 us

profile of v1, /device:TPU:25, one launch (start us, length us, event | category | flops | bytes accessed | tf_op | source)
XLA Modules:
  0.0 120.3 jit_solution(9792966809927727809)
XLA Ops:
  0.7 0.7 concatenate.3
  1.3 0.6 broadcast_in_dim.7.meta_ref
  1.9 116.3 %routed_attention.1 = bf16[384,1024]{1,0:T(8,128)(2,1)} custom-call(s32[8,512]{1,0:T(8,128)} %broadcast_in_dim.7.meta_ref, bf16[1536,1024]{1,0:T(8,128)(2,1)} %hidden_ref.1, f32[1,4096]{1,0:T(1,128)} %bitcast.3, bf16[4096,1024]{1,0:T(8,128)(2,1)} %wq_ref.1, bf16[1024,4096]{1,0:T(8,128)(2,1)} %wo_ref.1, bf16[1536,256]{1,0:T(8,128)(2,1)} %key_ref.1, ...), custom_call_target="tpu_custom_call" | custom-call | tf_op jit(solution)/shard_map/routed_attention/pallas_call | solution.py:351
  118.3 2.1 %copy.11 = bf16[384,1024]{1,0:T(8,128)(2,1)} copy(bf16[384,1024]{1,0:T(8,128)(2,1)} %routed_attention.1) | data formatting | bytes 1572864

commit v2 on v1

v2 whole, which is shorter than its diff:
```python
import functools
import math

import jax
import jax.numpy as jnp
from jax import lax
from jax.experimental import pallas as pl
from jax.experimental.pallas import tpu as pltpu
from jax.sharding import PartitionSpec as P

HEAD_SIZE = 128
M_DEV = 96
CHUNKS = 3
LANES = 128
TILE = 256

EPS = 1e-05
ROPE_BASE = 500000.0
NEG_FLOOR = -1e30
MESH = pl.DeviceIdType.MESH
F32 = jnp.float32
BF16 = jnp.bfloat16
I32 = jnp.int32


def iota(shape, dim):
    return lax.broadcasted_iota(I32, shape, dim)


def flip_bits(index, step, count):
    out, bit = 0, 1
    while bit < count:
        out = out + bit * (((index // bit) % 2 + (step // bit) % 2) % 2)
        bit *= 2
    return out


def kernel(
    n, nh, bucket,
    pos_ref, count_ref, hidden_ref, gain_ref, wq_ref, wo_ref, key_ref, val_ref,
    out_ref,
    hid, wq, wo, kbuf, vbuf, vext,
    meta, meta_all, onehot, send_rows, recv_rows, feats, normed, q_all,
    o_send, ml_send, o_recv, ml_recv, mixed, part_send, part_recv, upd, back_send, back_recv,
    load_sem, meta_s, meta_r, rows_s, rows_r, feat_s, feat_r, q_s, q_r, pass_s,
    o_s, o_r, ml_s, ml_r, part_s, part_r, back_s, back_r,
):
    seq_dev, width = hid.shape
    slots = pos_ref.shape[1]
    kv_local = key_ref.shape[1] // HEAD_SIZE
    q_cols = wq.shape[1]
    q_local = q_cols // HEAD_SIZE
    repeat = q_local // kv_local
    group = n * CHUNKS
    rows_c = M_DEV // CHUNKS
    per_chunk = n * bucket
    entries = CHUNKS * per_chunk
    low, bits = bucket - 1, int(math.log2(bucket))
    pairs = n // 2
    me = lax.axis_index("seq")
    hme = lax.axis_index("head")

    def load(i, src, dst):
        return pltpu.make_async_copy(src, dst, load_sem.at[i])

    loads = [
        load(0, hidden_ref, hid), load(1, val_ref, vbuf), load(2, wq_ref, wq),
        load(3, key_ref, kbuf), load(4, wo_ref, wo),
    ]
    loads[0].start()

    barrier = pltpu.get_barrier_semaphore()
    for step in range(1, n):
        pl.semaphore_signal(
            barrier, inc=1, device_id=(flip_bits(me, step, n), hme), device_id_type=MESH
        )
    for step in range(1, nh):
        pl.semaphore_signal(
            barrier, inc=1, device_id=(me, (hme + step) % nh), device_id_type=MESH
        )
    meta[:, 0:slots] = jnp.broadcast_to(pos_ref[...], (8, slots))
    meta[:, slots:] = jnp.broadcast_to(count_ref[...], (8, LANES))
    pl.semaphore_wait(barrier, n - 1 + nh - 1)

    def seq_copy(src, dst, send, recv, peer):
        return pltpu.make_async_remote_copy(
            src_ref=src, dst_ref=dst, send_sem=send, recv_sem=recv,
            device_id=(peer, hme), device_id_type=MESH,
        )

    def head_copy(src, dst, send, recv, peer):
        return pltpu.make_async_remote_copy(
            src_ref=src, dst_ref=dst, send_sem=send, recv_sem=recv,
            device_id=(me, peer), device_id_type=MESH,
        )

    def meta_copy(peer, slot):
        return seq_copy(meta, meta_all.at[slot], meta_s.at[peer], meta_r.at[slot], peer)

    def rows_copy(c, peer, slot):
        return seq_copy(
            send_rows.at[c, peer], recv_rows.at[c, slot], rows_s.at[c, peer],
            rows_r.at[c, slot], peer,
        )

    def feat_copy(c, peer, slot):
        return head_copy(
            feats.at[c, hme], feats.at[c, slot], feat_s.at[c, peer], feat_r.at[c, slot], peer
        )

    def q_copy(c, peer, slot):
        return seq_copy(
            q_all.at[c, me], q_all.at[c, slot], q_s.at[c, peer], q_r.at[c, slot], peer
        )

    def pass_copy(c, slot):
        return seq_copy(
            q_all.at[c, slot], q_all.at[c, slot], pass_s.at[c, slot], q_r.at[c, slot], sibling
        )

    def o_copy(c, peer, slot):
        return seq_copy(
            o_send.at[c, peer], o_recv.at[c, slot], o_s.at[c, peer], o_r.at[c, slot], peer
        )

    def ml_copy(c, peer, slot):
        return seq_copy(
            ml_send.at[c, peer], ml_recv.at[c, slot], ml_s.at[c, peer], ml_r.at[c, slot], peer
        )

    def part_copy(c, peer, slot):
        return head_copy(
            part_send.at[c, peer], part_recv.at[c, slot], part_s.at[c, peer],
            part_r.at[c, slot], peer,
        )

    def back_copy(c, peer, slot):
        return seq_copy(
            back_send.at[c, peer], back_recv.at[c, slot], back_s.at[c, peer],
            back_r.at[c, slot], peer,
        )

    sibling = flip_bits(me, 1, n)
    peers = [flip_bits(me, step, n) for step in range(n - 1, 0, -1)]
    cores = [flip_bits(me, step, n) for step in range(n - 2, 0, -2)]
    heads = [(hme + step) % nh for step in range(1, nh)]

    for peer in peers:
        meta_copy(peer, me).start()
    meta_all[me] = meta[...]
    loads[0].wait()
    for copy in loads[1:]:
        copy.start()
    upd[...] = jnp.zeros(upd.shape, BF16)
    for peer in peers:
        meta_copy(peer, peer).wait_recv()

    counts = [meta_all[s, 0:1, slots : slots + 1] for s in range(n)]
    offs, total = [], jnp.zeros((1, 1), I32)
    my_off = jnp.zeros((1, 1), I32)
    my_count = meta[0:1, slots : slots + 1]
    for s in range(n):
        offs.append(total)
        my_off = my_off + counts[s] * jnp.where(me > s, 1, 0)
        total = total + counts[s]

    def split(offset):
        whole = jnp.floor((offset.astype(F32) + 0.5) * (1.0 / group)).astype(I32)
        return whole, offset - whole * group

    parts = [split(offset) for offset in offs]
    my_rest = split(my_off)[1]

    def first_slot(kind, rest):
        return kind - rest + jnp.where(kind < rest, group, 0)

    def bucket_of(s, kind):
        whole, rest = parts[s]
        return whole + jnp.where(kind < rest, 1, 0), first_slot(kind, rest)

    my_pos = meta[0:1, 0:slots]
    for c in range(CHUNKS):
        entry = iota((per_chunk, slots), 0) + c * per_chunk
        slot = (entry & low) * group + first_slot(entry >> bits, my_rest)
        at = jnp.where(iota((per_chunk, slots), 1) == slot, my_pos, 0).astype(F32)
        place = jnp.sum(at, axis=1, keepdims=True)
        token = iota((per_chunk, seq_dev), 1).astype(F32)
        onehot[c * per_chunk : (c + 1) * per_chunk, :] = jnp.where(
            token == place, 1.0, 0.0
        ).astype(BF16)

    def pick(t, _):
        cols = pl.ds(pl.multiple_of(t * TILE, TILE), TILE)
        rows = jnp.dot(onehot[...], hid[:, cols], preferred_element_type=F32)
        send_rows[:, :, :, cols] = rows.astype(BF16).reshape(CHUNKS, n, bucket, TILE)
        return 0

    lax.fori_loop(0, width // TILE, pick, 0)
    for c in range(CHUNKS):
        for peer in peers:
            rows_copy(c, peer, me).start()
    for c in range(CHUNKS):
        recv_rows[c, me] = send_rows[c, me]

    def positions(c, d):
        row = iota((rows_c, slots), 0) * group + (c * n + d)
        lane = iota((rows_c, slots), 1)
        found = jnp.zeros((rows_c, slots), I32)
        for s in range(n):
            hit = (lane + offs[s] == row) & (lane < counts[s])
            found = jnp.where(hit, meta_all[s, 0:1, 0:slots] + s * seq_dev, found)
        return jnp.sum(found.astype(F32), axis=1, keepdims=True)

    lane = iota((rows_c, LANES), 1)
    half = HEAD_SIZE // 2
    freq = jnp.exp((-math.log(ROPE_BASE) * 2.0 / HEAD_SIZE) * (lane % half).astype(F32))
    turns = []
    for c in range(CHUNKS):
        angle = positions(c, me) * freq
        sine = jnp.sin(angle)
        turns.append((jnp.cos(angle), jnp.where(lane < half, -sine, sine)))
    loads[1].wait()
    for g in range(kv_local):
        vext[g, :, 0:HEAD_SIZE] = vbuf[:, g * HEAD_SIZE : (g + 1) * HEAD_SIZE]
        vext[g, :, HEAD_SIZE : 2 * HEAD_SIZE] = jnp.ones((seq_dev, HEAD_SIZE), BF16)

    def place_rows(c):
        row = iota((rows_c, per_chunk), 0)
        entry = iota((rows_c, per_chunk), 1)
        k, source = entry & low, entry >> bits
        placing = jnp.zeros((rows_c, per_chunk), F32)
        for s in range(n):
            base, first = bucket_of(s, c * n + me)
            hit = (source == s) & (row == base + k) & (k * group + first < counts[s])
            placing = jnp.where(hit, 1.0, placing)
        placing = placing.astype(BF16)
        for peer in peers:
            rows_copy(c, peer, peer).wait_recv()
        gathered = recv_rows[c].reshape(per_chunk, width)
        feats[c, hme] = jnp.dot(placing, gathered, preferred_element_type=F32).astype(BF16)
        for peer in heads:
            feat_copy(c, peer, hme).start()

    scale = 1.0 / math.sqrt(HEAD_SIZE)

    def query(c):
        for peer in heads:
            feat_copy(c, peer, peer).wait_recv()
        square = jnp.zeros((rows_c, 1), F32)
        for h in range(nh):
            wide = feats[c, h].astype(F32)
            square = square + jnp.sum(wide * wide, axis=1, keepdims=True)
        inv_rms = lax.rsqrt(square * (1.0 / (nh * width)) + EPS)
        for h in range(nh):
            gain = gain_ref[0:1, h * width : (h + 1) * width]
            normed[:, h * width : (h + 1) * width] = (
                feats[c, h].astype(F32) * inv_rms * gain
            ).astype(BF16)
        cosine, sine = turns[c]

        def project(t, _):
            cols = pl.ds(pl.multiple_of(t * TILE, TILE), TILE)
            raw = jnp.dot(normed[...], wq[:, cols], preferred_element_type=F32)
            turned = []
            for i in range(TILE // HEAD_SIZE):
                one = raw[:, i * HEAD_SIZE : (i + 1) * HEAD_SIZE]
                turned.append((one * cosine + pltpu.roll(one, half, 1) * sine) * scale)
            q_all[c, me, :, cols] = jnp.concatenate(turned, axis=1).astype(BF16)
            return 0

        lax.fori_loop(0, q_cols // TILE, project, 0)
        for peer in cores + [sibling]:
            q_copy(c, peer, me).start()

    token = (me * seq_dev + iota((1, seq_dev), 1)).astype(F32)

    def attend(c, start, stop):
        def one(step, _):
            pair = (pairs - step) % pairs
            ahead = pairs - step - 1
            both_d = [flip_bits(me, 2 * pair, n), flip_bits(me, 2 * pair + 1, n)]
            next_d = flip_bits(me, 2 * ahead, n)

            @pl.when(step == 0)
            def _():
                q_copy(c, sibling, sibling).wait_recv()

            @pl.when(step > 0)
            def _():
                q_copy(c, both_d[1], both_d[1]).wait_recv()

            def hand_on():
                @pl.when(ahead > 0)
                def _():
                    q_copy(c, next_d, next_d).wait_recv()
                    pass_copy(c, next_d).start()

            if c > 0:
                hand_on()
            pos = [positions(c, d) for d in both_d]
            bound = jnp.concatenate([pos[0]] * repeat + [pos[1]] * repeat, axis=0)
            stats = [jnp.zeros((rows_c, LANES), F32) for _ in both_d]
            for g in range(kv_local):
                rows = jnp.concatenate(
                    [
                        q_all[c, d, :, (g * repeat + i) * HEAD_SIZE : (g * repeat + i + 1) * HEAD_SIZE]
                        for d in both_d
                        for i in range(repeat)
                    ],
                    axis=0,
                )
                score = lax.dot_general(
                    rows, kbuf[:, g * HEAD_SIZE : (g + 1) * HEAD_SIZE],
                    (((1,), (1,)), ((), ())), preferred_element_type=F32,
                )
                score = jnp.where(token <= bound, score, NEG_FLOOR)
                peak = jnp.max(score, axis=1, keepdims=True)
                weight = jnp.exp(score - peak).astype(BF16)
                both = jnp.dot(weight, vext[g], preferred_element_type=F32)
                for j, d in enumerate(both_d):
                    for i in range(repeat):
                        head = g * repeat + i
                        at = (j * repeat + i) * rows_c
                        part = slice(at, at + rows_c)
                        o_send[c, d, :, head * HEAD_SIZE : (head + 1) * HEAD_SIZE] = (
                            both[part, 0:HEAD_SIZE].astype(BF16)
                        )
                        stats[j] = jnp.where(lane == head, peak[part], stats[j])
                        stats[j] = jnp.where(
                            lane == q_local + head, both[part, HEAD_SIZE:], stats[j]
                        )
            for j, d in enumerate(both_d):
                ml_send[c, d] = stats[j]

            @pl.when(step > 0)
            def _():
                o_copy(c, both_d[0], me).start()
                ml_copy(c, both_d[0], me).start()

            o_copy(c, both_d[1], me).start()
            ml_copy(c, both_d[1], me).start()
            if c == 0:
                hand_on()
            return 0

        lax.fori_loop(start, stop, one, 0)

    def join(c):
        o_recv[c, me] = o_send[c, me]
        ml_recv[c, me] = ml_send[c, me]
        for peer in peers:
            ml_copy(c, peer, peer).wait_recv()
            o_copy(c, peer, peer).wait_recv()
        top = ml_recv[c, 0]
        for s in range(1, n):
            top = jnp.maximum(top, ml_recv[c, s])
        denom = jnp.zeros((rows_c, LANES), F32)
        shares = []
        for s in range(n):
            aligned = pltpu.roll(ml_recv[c, s], LANES - q_local, 1)
            shares.append(jnp.exp(ml_recv[c, s] - top))
            denom = denom + shares[s] * aligned
        shares = [share / denom for share in shares]
        for head in range(q_local):
            cols = slice(head * HEAD_SIZE, (head + 1) * HEAD_SIZE)
            joined = jnp.zeros((rows_c, HEAD_SIZE), F32)
            for s in range(n):
                joined = joined + shares[s][:, head : head + 1] * o_recv[c, s, :, cols].astype(F32)
            mixed[:, cols] = joined.astype(BF16)
        for peer in heads + [hme]:

            def block(t, _):
                cols = pl.ds(pl.multiple_of(t * TILE, TILE), TILE)
                src = pl.ds(pl.multiple_of(peer * width + t * TILE, TILE), TILE)
                part_send[c, peer, :, cols] = jnp.dot(
                    mixed[...], wo[:, src], preferred_element_type=F32
                ).astype(BF16)
                return 0

            lax.fori_loop(0, width // TILE, block, 0)
            if peer is not hme:
                part_copy(c, peer, hme).start()
        part_recv[c, hme] = part_send[c, hme]

    def give_back(c):
        entry = iota((per_chunk, LANES), 0)
        k, source = entry & low, entry >> bits
        place = iota((per_chunk, LANES), 1)
        sending = jnp.zeros((per_chunk, LANES), F32)
        for s in range(n):
            base, first = bucket_of(s, c * n + me)
            hit = (source == s) & (place == base + k) & (k * group + first < counts[s])
            sending = jnp.where(hit, 1.0, sending)
        for peer in heads:
            part_copy(c, peer, peer).wait_recv()
        update = part_recv[c, 0].astype(F32)
        for h in range(1, nh):
            update = update + part_recv[c, h].astype(F32)
        upd[0:rows_c, :] = update.astype(BF16)
        back = jnp.dot(sending.astype(BF16), upd[...], preferred_element_type=F32)
        back_send[c] = back.astype(BF16).reshape(n, bucket, width)
        for peer in peers:
            back_copy(c, peer, me).start()
        back_recv[c, me] = back_send[c, me]

    for c in range(CHUNKS):
        place_rows(c)
    loads[2].wait()
    loads[3].wait()
    query(0)
    attend(0, 0, 1)
    query(1)
    attend(0, 1, pairs)
    query(2)
    attend(1, 0, pairs)
    loads[4].wait()
    join(0)
    attend(2, 0, pairs // 2)
    join(1)
    attend(2, pairs // 2, pairs)
    give_back(0)
    join(2)
    give_back(1)
    give_back(2)

    entry = iota((slots, entries), 1)
    source = (entry & low) * group + first_slot(entry >> bits, my_rest)
    slot = iota((slots, entries), 0)
    restoring = jnp.where((source == slot) & (slot < my_count), 1.0, 0.0).astype(BF16)
    for c in range(CHUNKS):
        for peer in peers:
            back_copy(c, peer, peer).wait_recv()
    out_ref[...] = jnp.dot(
        restoring, back_recv[...].reshape(entries, width), preferred_element_type=F32
    ).astype(BF16)

    for peer in peers:
        meta_copy(peer, me).wait_send()
    for c in range(CHUNKS):
        for peer in peers:
            rows_copy(c, peer, me).wait_send()
            o_copy(c, peer, me).wait_send()
            ml_copy(c, peer, me).wait_send()
            back_copy(c, peer, me).wait_send()
        for peer in cores + [sibling]:
            q_copy(c, peer, me).wait_send()
        for peer in cores:
            pass_copy(c, peer).wait_send()
        for peer in heads:
            feat_copy(c, peer, hme).wait_send()
            part_copy(c, peer, hme).wait_send()


def body(hidden, norm_gain, w_query, w_out, keys, values, cand_count, cand_pos):
    n, nh = lax.axis_size("seq"), lax.axis_size("head")
    seq_dev, width = hidden.shape
    slots = cand_pos.shape[0]
    bucket = -(-slots // (n * CHUNKS))
    bucket = -(-bucket // 16) * 16
    per_chunk = n * bucket
    rows_c = M_DEV // CHUNKS
    q_cols = w_query.shape[1]
    kv_local = keys.shape[1] // HEAD_SIZE
    seq_sem = pltpu.SemaphoreType.DMA((CHUNKS, n))
    head_sem = pltpu.SemaphoreType.DMA((CHUNKS, nh))
    one_sem = pltpu.SemaphoreType.DMA((n,))
    vmem, hbm = pl.BlockSpec(memory_space=pltpu.VMEM), pl.BlockSpec(memory_space=pl.ANY)
    return pl.pallas_call(
        functools.partial(kernel, n, nh, bucket),
        out_shape=jax.ShapeDtypeStruct((slots, width), BF16),
        in_specs=[vmem, vmem, hbm, vmem, hbm, hbm, hbm, hbm],
        out_specs=vmem,
        scratch_shapes=[
            pltpu.VMEM(hidden.shape, BF16),
            pltpu.VMEM(w_query.shape, BF16),
            pltpu.VMEM(w_out.shape, BF16),
            pltpu.VMEM(keys.shape, BF16),
            pltpu.VMEM(values.shape, BF16),
            pltpu.VMEM((kv_local, seq_dev, 2 * HEAD_SIZE), BF16),
            pltpu.VMEM((8, slots + LANES), I32),
            pltpu.VMEM((n, 8, slots + LANES), I32),
            pltpu.VMEM((CHUNKS * per_chunk, seq_dev), BF16),
            pltpu.VMEM((CHUNKS, n, bucket, width), BF16),
            pltpu.VMEM((CHUNKS, n, bucket, width), BF16),
            pltpu.VMEM((CHUNKS, nh, rows_c, width), BF16),
            pltpu.VMEM((rows_c, nh * width), BF16),
            pltpu.VMEM((CHUNKS, n, rows_c, q_cols), BF16),
            pltpu.VMEM((CHUNKS, n, rows_c, q_cols), BF16),
            pltpu.VMEM((CHUNKS, n, rows_c, LANES), F32),
            pltpu.VMEM((CHUNKS, n, rows_c, q_cols), BF16),
            pltpu.VMEM((CHUNKS, n, rows_c, LANES), F32),
            pltpu.VMEM((rows_c, q_cols), BF16),
            pltpu.VMEM((CHUNKS, nh, rows_c, width), BF16),
            pltpu.VMEM((CHUNKS, nh, rows_c, width), BF16),
            pltpu.VMEM((LANES, width), BF16),
            pltpu.VMEM((CHUNKS, n, bucket, width), BF16),
            pltpu.VMEM((CHUNKS, n, bucket, width), BF16),
            pltpu.SemaphoreType.DMA((5,)),
            one_sem, one_sem, seq_sem, seq_sem, head_sem, head_sem, seq_sem, seq_sem, seq_sem,
            seq_sem, seq_sem, seq_sem, seq_sem, head_sem, head_sem, seq_sem, seq_sem,
        ],
        compiler_params=pltpu.CompilerParams(
            collective_id=0, has_side_effects=True, vmem_limit_bytes=60 * 1024 * 1024
        ),
        name="routed_attention",
    )(
        cand_pos[None, :], cand_count[None, :], hidden, norm_gain[None, :],
        w_query, w_out, keys, values,
    )


def solution(mesh):
    in_specs = (
        P("seq", "head"),
        P(),
        P(None, "head"),
        P("head", None),
        P("seq", "head"),
        P("seq", "head"),
        P("seq"),
        P("seq"),
    )
    out_specs = P("seq", "head")
    return jax.shard_map(body, mesh=mesh, in_specs=in_specs, out_specs=out_specs, check_vma=False)
```

time: 121 us -> 96.2 us (0.80)
  the two profiles are of different devices: /device:TPU:25 before, /device:TPU:0 now
where the time goes in v2:
time: 96.2 us; the launch traced here: 96 us
  Pallas kernels  92 us (96%)
  local copies, waits for them, and re-layouts  3.31 us (3%)
    pallas_call x1, Pallas kernels, body(): pl.pallas_call(functools.partial(kernel, n, nh, bucket), out_shape=jax.Sh...  92 us
    unnamed x1, local copies, waits for them, and re-layouts  2.06 us

profile of v2, /device:TPU:0, one launch (start us, length us, event | category | flops | bytes accessed | tf_op | source)
XLA Modules:
  0.0 96.0 jit_solution(304882946839368422)
XLA Ops:
  0.7 1.2 %broadcast_in_dim.9.pos_ref = s32[1,384]{1,0:T(1,128)} reshape(s32[384]{0:T(512)} %param.15) | data formatting | bytes 3072 | tf_op jit(solution)/shard_map/broadcast_in_dim | solution.py:507
  1.9 92.0 %routed_attention.1 = bf16[384,1024]{1,0:T(8,128)(2,1)} custom-call(s32[1,384]{1,0:T(1,128)} %broadcast_in_dim.9.pos_ref, s32[1,1]{1,0:T(1,128)} %bitcast.2.count_ref, bf16[1536,1024]{1,0:T(8,128)(2,1)} %hidden_ref.1, f32[1,4096]{1,0:T(1,128)} %bitcast.3, bf16[4096,1024]{1,0:T(8,128)(2,1)} %wq_ref.1, bf16[1024,4096]{1,0:T(8,128)(2,1)} %wo_ref.1, ...), custom_call_target="tpu_custom_call" | custom-call | tf_op jit(solution)/shard_map/routed_attention/pallas_call | solution.py:468
  93.9 2.1 %copy.11 = bf16[384,1024]{1,0:T(8,128)(2,1)} copy(bf16[384,1024]{1,0:T(8,128)(2,1)} %routed_attention.1) | data formatting | bytes 1572864

commit v3 on v2

--- a/solution.py
+++ b/solution.py
@@ -39,14 +39,14 @@
     n, nh, bucket,
     pos_ref, count_ref, hidden_ref, gain_ref, wq_ref, wo_ref, key_ref, val_ref,
     out_ref,
-    hid, wq, wo, kbuf, vbuf, vext,
+    hid, wq, wo, kbuf, vbuf, kext, vext, pos_all,
     meta, meta_all, onehot, send_rows, recv_rows, feats, normed, q_all,
     o_send, ml_send, o_recv, ml_recv, mixed, part_send, part_recv, upd, back_send, back_recv,
     load_sem, meta_s, meta_r, rows_s, rows_r, feat_s, feat_r, q_s, q_r, pass_s,
     o_s, o_r, ml_s, ml_r, part_s, part_r, back_s, back_r,
 ):
     seq_dev, width = hid.shape
-    slots = pos_ref.shape[1]
+    slots = pos_ref.shape[0]
     kv_local = key_ref.shape[1] // HEAD_SIZE
     q_cols = wq.shape[1]
     q_local = q_cols // HEAD_SIZE
@@ -64,8 +64,8 @@
         return pltpu.make_async_copy(src, dst, load_sem.at[i])
 
     loads = [
-        load(0, hidden_ref, hid), load(1, val_ref, vbuf), load(2, wq_ref, wq),
-        load(3, key_ref, kbuf), load(4, wo_ref, wo),
+        load(0, hidden_ref, hid), load(1, val_ref, vbuf), load(2, key_ref, kbuf),
+        load(3, wq_ref, wq), load(4, wo_ref, wo),
     ]
     loads[0].start()
 
@@ -78,7 +78,7 @@
         pl.semaphore_signal(
             barrier, inc=1, device_id=(me, (hme + step) % nh), device_id_type=MESH
         )
-    meta[:, 0:slots] = jnp.broadcast_to(pos_ref[...], (8, slots))
+    meta[:, 0:slots] = jnp.broadcast_to(pos_ref[...].reshape(1, slots), (8, slots))
     meta[:, slots:] = jnp.broadcast_to(count_ref[...], (8, LANES))
     pl.semaphore_wait(barrier, n - 1 + nh - 1)
 
@@ -185,21 +185,17 @@
         at = jnp.where(iota((per_chunk, slots), 1) == slot, my_pos, 0).astype(F32)
         place = jnp.sum(at, axis=1, keepdims=True)
         token = iota((per_chunk, seq_dev), 1).astype(F32)
-        onehot[c * per_chunk : (c + 1) * per_chunk, :] = jnp.where(
-            token == place, 1.0, 0.0
-        ).astype(BF16)
-
-    def pick(t, _):
-        cols = pl.ds(pl.multiple_of(t * TILE, TILE), TILE)
-        rows = jnp.dot(onehot[...], hid[:, cols], preferred_element_type=F32)
-        send_rows[:, :, :, cols] = rows.astype(BF16).reshape(CHUNKS, n, bucket, TILE)
-        return 0
-
-    lax.fori_loop(0, width // TILE, pick, 0)
-    for c in range(CHUNKS):
+        onehot[...] = jnp.where(token == place, 1.0, 0.0).astype(BF16)
+
+        def pick(t, _):
+            cols = pl.ds(pl.multiple_of(t * TILE, TILE), TILE)
+            rows = jnp.dot(onehot[...], hid[:, cols], preferred_element_type=F32)
+            send_rows[c, :, :, cols] = rows.astype(BF16).reshape(n, bucket, TILE)
+            return 0
+
+        lax.fori_loop(0, width // TILE, pick, 0)
         for peer in peers:
             rows_copy(c, peer, me).start()
-    for c in range(CHUNKS):
         recv_rows[c, me] = send_rows[c, me]
 
     def positions(c, d):
@@ -214,13 +210,22 @@
     lane = iota((rows_c, LANES), 1)
     half = HEAD_SIZE // 2
     freq = jnp.exp((-math.log(ROPE_BASE) * 2.0 / HEAD_SIZE) * (lane % half).astype(F32))
-    turns = []
-    for c in range(CHUNKS):
-        angle = positions(c, me) * freq
+
+    def note_positions(c):
+        def one(d, _):
+            pos_all[c, d] = jnp.broadcast_to(positions(c, d), (rows_c, LANES))
+            return 0
+
+        lax.fori_loop(0, n, one, 0)
+        angle = pos_all[c, me] * freq
         sine = jnp.sin(angle)
-        turns.append((jnp.cos(angle), jnp.where(lane < half, -sine, sine)))
+        return jnp.cos(angle), jnp.where(lane < half, -sine, sine)
+
+    turns = [note_positions(0)]
     loads[1].wait()
+    loads[2].wait()
     for g in range(kv_local):
+        kext[g] = kbuf[:, g * HEAD_SIZE : (g + 1) * HEAD_SIZE].T
         vext[g, :, 0:HEAD_SIZE] = vbuf[:, g * HEAD_SIZE : (g + 1) * HEAD_SIZE]
         vext[g, :, HEAD_SIZE : 2 * HEAD_SIZE] = jnp.ones((seq_dev, HEAD_SIZE), BF16)
 
@@ -241,7 +246,7 @@
         for peer in heads:
             feat_copy(c, peer, hme).start()
 
-    scale = 1.0 / math.sqrt(HEAD_SIZE)
+    scale = math.log2(math.e) / math.sqrt(HEAD_SIZE)
 
     def query(c):
         for peer in heads:
@@ -297,7 +302,7 @@
 
             if c > 0:
                 hand_on()
-            pos = [positions(c, d) for d in both_d]
+            pos = [pos_all[c, d][:, 0:1] for d in both_d]
             bound = jnp.concatenate([pos[0]] * repeat + [pos[1]] * repeat, axis=0)
             stats = [jnp.zeros((rows_c, LANES), F32) for _ in both_d]
             for g in range(kv_local):
@@ -309,13 +314,10 @@
                     ],
                     axis=0,
                 )
-                score = lax.dot_general(
-                    rows, kbuf[:, g * HEAD_SIZE : (g + 1) * HEAD_SIZE],
-                    (((1,), (1,)), ((), ())), preferred_element_type=F32,
-                )
+                score = jnp.dot(rows, kext[g], preferred_element_type=F32)
                 score = jnp.where(token <= bound, score, NEG_FLOOR)
                 peak = jnp.max(score, axis=1, keepdims=True)
-                weight = jnp.exp(score - peak).astype(BF16)
+                weight = jnp.exp2(score - peak).astype(BF16)
                 both = jnp.dot(weight, vext[g], preferred_element_type=F32)
                 for j, d in enumerate(both_d):
                     for i in range(repeat):
@@ -358,7 +360,7 @@
         shares = []
         for s in range(n):
             aligned = pltpu.roll(ml_recv[c, s], LANES - q_local, 1)
-            shares.append(jnp.exp(ml_recv[c, s] - top))
+            shares.append(jnp.exp2(ml_recv[c, s] - top))
             denom = denom + shares[s] * aligned
         shares = [share / denom for share in shares]
         for head in range(q_local):
@@ -405,7 +407,8 @@
 
     for c in range(CHUNKS):
         place_rows(c)
-    loads[2].wait()
+        if c > 0:
+            turns.append(note_positions(c))
     loads[3].wait()
     query(0)
     attend(0, 0, 1)
@@ -476,10 +479,12 @@
             pltpu.VMEM(w_out.shape, BF16),
             pltpu.VMEM(keys.shape, BF16),
             pltpu.VMEM(values.shape, BF16),
+            pltpu.VMEM((kv_local, HEAD_SIZE, seq_dev), BF16),
             pltpu.VMEM((kv_local, seq_dev, 2 * HEAD_SIZE), BF16),
+            pltpu.VMEM((CHUNKS, n, rows_c, LANES), F32),
             pltpu.VMEM((8, slots + LANES), I32),
             pltpu.VMEM((n, 8, slots + LANES), I32),
-            pltpu.VMEM((CHUNKS * per_chunk, seq_dev), BF16),
+            pltpu.VMEM((per_chunk, seq_dev), BF16),
             pltpu.VMEM((CHUNKS, n, bucket, width), BF16),
             pltpu.VMEM((CHUNKS, n, bucket, width), BF16),
             pltpu.VMEM((CHUNKS, nh, rows_c, width), BF16),
@@ -504,7 +509,7 @@
         ),
         name="routed_attention",
     )(
-        cand_pos[None, :], cand_count[None, :], hidden, norm_gain[None, :],
+        cand_pos, cand_count[None, :], hidden, norm_gain[None, :],
         w_query, w_out, keys, values,
     )
 

time: 96.2 us -> 94.5 us (0.982)
  local copies, waits for them, and re-layouts: 3.31 us -> 2.06 us
    broadcast_in_dim x1 -> x0, local copies, waits for them, and re-layouts: 1.25 us -> none  [body(): cand_pos[None, :]]
where the time goes in v3:
time: 94.5 us; the launch traced here: 94.2 us
  Pallas kernels  91.5 us (97%)
  local copies, waits for them, and re-layouts  2.06 us (2%)
    pallas_call x1, Pallas kernels, body(): pl.pallas_call(functools.partial(kernel, n, nh, bucket), out_shape=jax.Sh...  91.5 us
    unnamed x1, local copies, waits for them, and re-layouts  2.06 us

profile of v3, /device:TPU:0, one launch (start us, length us, event | category | flops | bytes accessed | tf_op | source)
XLA Modules:
  0.0 94.2 jit_solution(11604432009176396208)
XLA Ops:
  0.7 91.5 %routed_attention.1 = bf16[384,1024]{1,0:T(8,128)(2,1)} custom-call(s32[384]{0:T(512)} %pos_ref.1, s32[1,1]{1,0:T(1,128)} %bitcast.2.count_ref, bf16[1536,1024]{1,0:T(8,128)(2,1)} %hidden_ref.1, f32[1,4096]{1,0:T(1,128)} %bitcast.3, bf16[4096,1024]{1,0:T(8,128)(2,1)} %wq_ref.1, bf16[1024,4096]{1,0:T(8,128)(2,1)} %wo_ref.1, bf16[1536,256]{1,0:T(8,128)(2,1)} %key_ref.1, ...), custom_call_target="tpu_custom_call" | custom-call | tf_op jit(solution)/shard_map/routed_attention/pallas_call | solution.py:471
  92.1 2.1 %copy.11 = bf16[384,1024]{1,0:T(8,128)(2,1)} copy(bf16[384,1024]{1,0:T(8,128)(2,1)} %routed_attention.1) | data formatting | bytes 1572864

commit v4 on v3

--- a/solution.py
+++ b/solution.py
@@ -57,6 +57,7 @@
     entries = CHUNKS * per_chunk
     low, bits = bucket - 1, int(math.log2(bucket))
     pairs = n // 2
+    spread = LANES * 8 // rows_c
     me = lax.axis_index("seq")
     hme = lax.axis_index("head")
 
@@ -332,7 +333,10 @@
                             lane == q_local + head, both[part, HEAD_SIZE:], stats[j]
                         )
             for j, d in enumerate(both_d):
-                ml_send[c, d] = stats[j]
+                packed = stats[j][0:8]
+                for b in range(1, rows_c // 8):
+                    packed = packed + pltpu.roll(stats[j][8 * b : 8 * b + 8], b * spread, 1)
+                ml_send[c, d] = packed
 
             @pl.when(step > 0)
             def _():
@@ -346,6 +350,10 @@
             return 0
 
         lax.fori_loop(start, stop, one, 0)
+
+    def unpack(packed):
+        turned = [pltpu.roll(packed, LANES - b * spread, 1) for b in range(1, rows_c // 8)]
+        return jnp.concatenate([packed] + turned, axis=0)
 
     def join(c):
         o_recv[c, me] = o_send[c, me]
@@ -353,14 +361,15 @@
         for peer in peers:
             ml_copy(c, peer, peer).wait_recv()
             o_copy(c, peer, peer).wait_recv()
-        top = ml_recv[c, 0]
+        stat = [unpack(ml_recv[c, s]) for s in range(n)]
+        top = stat[0]
         for s in range(1, n):
-            top = jnp.maximum(top, ml_recv[c, s])
+            top = jnp.maximum(top, stat[s])
         denom = jnp.zeros((rows_c, LANES), F32)
         shares = []
         for s in range(n):
-            aligned = pltpu.roll(ml_recv[c, s], LANES - q_local, 1)
-            shares.append(jnp.exp2(ml_recv[c, s] - top))
+            aligned = pltpu.roll(stat[s], LANES - q_local, 1)
+            shares.append(jnp.exp2(stat[s] - top))
             denom = denom + shares[s] * aligned
         shares = [share / denom for share in shares]
         for head in range(q_local):
@@ -491,9 +500,9 @@
             pltpu.VMEM((rows_c, nh * width), BF16),
             pltpu.VMEM((CHUNKS, n, rows_c, q_cols), BF16),
             pltpu.VMEM((CHUNKS, n, rows_c, q_cols), BF16),
-            pltpu.VMEM((CHUNKS, n, rows_c, LANES), F32),
+            pltpu.VMEM((CHUNKS, n, 8, LANES), F32),
             pltpu.VMEM((CHUNKS, n, rows_c, q_cols), BF16),
-            pltpu.VMEM((CHUNKS, n, rows_c, LANES), F32),
+            pltpu.VMEM((CHUNKS, n, 8, LANES), F32),
             pltpu.VMEM((rows_c, q_cols), BF16),
             pltpu.VMEM((CHUNKS, nh, rows_c, width), BF16),
             pltpu.VMEM((CHUNKS, nh, rows_c, width), BF16),

time: 94.5 us -> 94.4 us (level)
  no operation moved by 1% of the time
where the time goes in v4:
time: 94.4 us; the launch traced here: 94.2 us
  Pallas kernels  91.5 us (97%)
  local copies, waits for them, and re-layouts  2.06 us (2%)
    pallas_call x1, Pallas kernels, body(): pl.pallas_call(functools.partial(kernel, n, nh, bucket), out_shape=jax.Sh...  91.5 us
    unnamed x1, local copies, waits for them, and re-layouts  2.06 us

profile of v4, /device:TPU:0, one launch (start us, length us, event | category | flops | bytes accessed | tf_op | source)
XLA Modules:
  0.0 94.2 jit_solution(5054079657329038687)
XLA Ops:
  0.7 91.5 %routed_attention.1 = bf16[384,1024]{1,0:T(8,128)(2,1)} custom-call(s32[384]{0:T(512)} %pos_ref.1, s32[1,1]{1,0:T(1,128)} %bitcast.2.count_ref, bf16[1536,1024]{1,0:T(8,128)(2,1)} %hidden_ref.1, f32[1,4096]{1,0:T(1,128)} %bitcast.3, bf16[4096,1024]{1,0:T(8,128)(2,1)} %wq_ref.1, bf16[1024,4096]{1,0:T(8,128)(2,1)} %wo_ref.1, bf16[1536,256]{1,0:T(8,128)(2,1)} %key_ref.1, ...), custom_call_target="tpu_custom_call" | custom-call | tf_op jit(solution)/shard_map/routed_attention/pallas_call | solution.py:480
  92.1 2.1 %copy.11 = bf16[384,1024]{1,0:T(8,128)(2,1)} copy(bf16[384,1024]{1,0:T(8,128)(2,1)} %routed_attention.1) | data formatting | bytes 1572864
